TPU v7x, 32 devices: a whole 2x2x4 slice. The times are simulated.
32 devices in a mesh: groups: 2 (over x), seq: 16 (over z, y, core).
Axes of the slice: x: 2, y: 2, z: 4, core: 2. Of those that a mesh axis runs over, the one named last changes fastest.
Arguments:
- xbc: bfloat16 [16384, 1408], P(('groups', 'seq')), parts along dimension 0, may hold values from -6 to 6
- dt_raw: float32 [40, 16384], P(None, ('groups', 'seq')), parts along dimension 1, may hold values from -6 to 6
- cotangent: bfloat16 [16384, 1280], P(('groups', 'seq')), parts along dimension 0, may hold values from -0.29882812 to 0.29882812
- conv_weight: float32 [4, 1408], replicated, may hold values from -3 to 3
- conv_bias: float32 [1408], replicated, may hold values from -3 to 3
- dt_bias: float32 [40], replicated, may hold values from -3 to 3
- a_log: float32 [40], replicated, may hold values from -14 to -2.9
- d_skip: float32 [40], replicated, may hold values from 0.25 to 2.5
Outputs:
- grad_xbc: bfloat16 [16384, 1408], P(('groups', 'seq')), parts along dimension 0
- grad_dt_raw: float32 [40, 16384], P(None, ('groups', 'seq')), parts along dimension 1
- grad_conv_weight: float32 [8, 1408], P('groups'), parts along dimension 0
- grad_conv_bias: float32 [2816], P('groups'), parts along dimension 0
- grad_dt_bias: float32 [80], P('groups'), parts along dimension 0
- grad_a_log: float32 [80], P('groups'), parts along dimension 0
- grad_d_skip: float32 [80], P('groups'), parts along dimension 0
There are 2 independent parts, one for each index of `groups`. A program takes and returns all parts, laid end to end along the dimension named above; an argument that names none is the same for every part. Nothing has to cross between parts.
All inputs are finite; a program needn't handle non-finite values.
Results may differ from a plain program's by a relative error of at most 0.011.
Values may be sent and summed in bfloat16 or wider, within the bound.
A program may use at most 192 MiB of HBM per device.

v0:
```python
import jax
import jax.numpy as jnp
from jax import lax
from jax.sharding import PartitionSpec as P

HEADS = 40
HEAD_DIM = 32
STATE = 64
BLOCK = 128


def prefix(array, axis, join, neutral):
    place = lax.axis_index(axis)
    gathered = jax.tree.map(
        lambda a, kind: lax.all_gather(a.astype(kind), axis), array, (jnp.bfloat16, jnp.bfloat16)
    )
    state = jax.tree.map(lambda a, e: jnp.zeros_like(a) + jnp.asarray(e, a.dtype), array, neutral)

    def one(hop, state):
        return join(
            state,
            jax.tree.map(
                lambda a, own: lax.dynamic_index_in_dim(a, hop, 0, False).astype(own.dtype),
                gathered,
                array,
            ),
        )

    return lax.fori_loop(0, place, one, state)


def carried_in(array, axis, combine, identity):
    length, place = (lax.axis_size(axis), lax.axis_index(axis))
    everything = jax.tree.map(
        lambda part, kind: lax.all_gather(part.astype(kind), axis),
        array,
        jax.tree.map(lambda a: jnp.bfloat16 if a.dtype == jnp.float32 else a.dtype, array),
    )
    start = jax.tree.map(
        lambda part, zero: jnp.broadcast_to(jnp.asarray(zero, part.dtype), part.shape),
        array,
        identity,
    )

    def hop(k, before):
        at = length - 1 - k
        reached = at > place
        new = combine(
            before, jax.tree.map(lambda part, own: part[at].astype(own.dtype), everything, array)
        )
        return jax.tree.map(lambda a, b: jnp.where(reached, a, b), new, before)

    return lax.fori_loop(0, length, hop, start)


def shifted(array, axis, by):
    length = lax.axis_size(axis)
    pairs = [(i, i + by) for i in range(length) if 0 <= i + by < length]
    return lax.ppermute(array, axis, pairs)


def prepare(block_rows, edge_rows, dt_raw, conv_weight, conv_bias, dt_bias, a_log):
    inner = HEADS * HEAD_DIM
    padded = jnp.concatenate([edge_rows, block_rows], axis=0)
    row_count = block_rows.shape[0]
    total = jnp.broadcast_to(conv_bias[None, :], (row_count, conv_bias.shape[0]))
    for offset in range(conv_weight.shape[0]):
        total = total + conv_weight[offset][None, :] * padded[offset : offset + row_count]
    activ = jax.nn.silu(total).astype(jnp.bfloat16)
    step_size = jax.nn.softplus(dt_raw + dt_bias[:, None])
    heads = step_size.shape[0]
    rate = -jnp.exp(a_log)[:, None] * step_size
    cumulated = jnp.cumsum(rate.reshape(heads, row_count // BLOCK, BLOCK), axis=2).reshape(
        heads, row_count
    )
    return (
        activ[:, :inner],
        activ[:, inner : inner + STATE],
        activ[:, inner + STATE :],
        step_size,
        cumulated,
    )


@jax.checkpoint
def intra_block(x_part, b_part, c_part, step_size, cumulated):
    row_count = x_part.shape[0]
    heads = step_size.shape[0]
    x_heads = x_part.reshape(row_count, heads, HEAD_DIM)
    inner_scores = jnp.dot(c_part, b_part.T, preferred_element_type=jnp.float32)
    causal = lax.broadcasted_iota(jnp.int32, (row_count, row_count), 0) >= lax.broadcasted_iota(
        jnp.int32, (row_count, row_count), 1
    )
    spread = cumulated[:, :, None] - cumulated[:, None, :]
    falloff = jnp.where(causal[None], jnp.exp(jnp.where(causal[None], spread, 0.0)), 0.0)
    weights = (inner_scores[None] * falloff * step_size[:, None, :]).astype(jnp.bfloat16)
    return jnp.einsum("hts,shp->thp", weights, x_heads, preferred_element_type=jnp.float32)


def block_outputs(x_part, b_part, c_part, step_size, cumulated, state_in, d_skip):
    row_count = x_part.shape[0]
    heads = step_size.shape[0]
    x_heads = x_part.reshape(row_count, heads, HEAD_DIM)
    local_term = intra_block(x_part, b_part, c_part, step_size, cumulated)
    carried_term = jnp.einsum(
        "tn,hnp->thp", c_part.astype(jnp.float32), state_in, precision=lax.Precision.HIGHEST
    )
    carried_term = carried_term * jnp.exp(cumulated).T[:, :, None]
    skip_term = d_skip[None, :, None] * x_heads.astype(jnp.float32)
    return (local_term + carried_term + skip_term).reshape(row_count, heads * HEAD_DIM)


def block_state(x_part, b_part, step_size, cumulated):
    row_count = x_part.shape[0]
    heads = step_size.shape[0]
    x_heads = x_part.reshape(row_count, heads, HEAD_DIM)
    weights = jnp.exp(cumulated[:, -1:] - cumulated) * step_size
    scaled = x_heads.astype(jnp.float32) * weights.T[:, :, None]
    state_piece = jnp.einsum(
        "tn,thp->hnp", b_part.astype(jnp.float32), scaled, precision=lax.Precision.HIGHEST
    )
    return (state_piece, jnp.exp(cumulated[:, -1]))


def to_blocks(x_part, b_part, c_part, step_size, cumulated):
    count = x_part.shape[0] // BLOCK
    heads = step_size.shape[0]
    return (
        x_part.reshape(count, BLOCK, x_part.shape[1]),
        b_part.reshape(count, BLOCK, b_part.shape[1]),
        c_part.reshape(count, BLOCK, c_part.shape[1]),
        step_size.reshape(heads, count, BLOCK).transpose(1, 0, 2),
        cumulated.reshape(heads, count, BLOCK).transpose(1, 0, 2),
    )


def outputs(x_part, b_part, c_part, step_size, cumulated, state_in, d_skip):
    row_count = x_part.shape[0]

    def outputs_advance(carried, pieces):
        x_blk, b_blk, c_blk, step_blk, cum_blk = pieces
        result = block_outputs(x_blk, b_blk, c_blk, step_blk, cum_blk, carried, d_skip)
        state_piece, decay = block_state(x_blk, b_blk, step_blk, cum_blk)
        return (decay[:, None, None] * carried + state_piece, result)

    final_state, results = lax.scan(
        outputs_advance, state_in, to_blocks(x_part, b_part, c_part, step_size, cumulated)
    )
    return results.reshape(row_count, x_part.shape[1])


def local_state(x_part, b_part, step_size, cumulated):
    heads = step_size.shape[0]

    def local_advance(carried, pieces):
        x_blk, b_blk, step_blk, cum_blk = pieces
        state_piece, decay = block_state(x_blk, b_blk, step_blk, cum_blk)
        return ((carried[0] * decay, decay[:, None, None] * carried[1] + state_piece), None)

    blocked = to_blocks(x_part, b_part, b_part, step_size, cumulated)
    start = (jnp.ones((heads,), jnp.float32), jnp.zeros((heads, STATE, HEAD_DIM), jnp.float32))
    final_pair, unused = lax.scan(
        local_advance, start, (blocked[0], blocked[1], blocked[3], blocked[4])
    )
    return (final_pair[1], final_pair[0])


def chain_combine(earlier, later):
    return (earlier[0] * later[0], later[0][:, None, None] * earlier[1] + later[1])


def pass_states(decay, state_piece):
    identity = (jnp.ones_like(decay), jnp.zeros_like(state_piece))
    return prefix((decay, state_piece), "seq", chain_combine, identity)[1]


def pass_adjoints(decay, adjoint_in):
    identity = (jnp.ones_like(decay), jnp.zeros_like(adjoint_in))
    return carried_in((decay, adjoint_in), "seq", chain_combine, identity)[1]


def local(xbc, dt_raw, cotangent, conv_weight, conv_bias, dt_bias, a_log, d_skip):
    row_count = xbc.shape[0]
    margin = conv_weight.shape[0] - 1
    edge_rows = shifted(xbc[row_count - margin :], "seq", 1)
    prepared, prep_back = jax.vjp(
        prepare,
        xbc.astype(jnp.float32),
        edge_rows.astype(jnp.float32),
        dt_raw,
        conv_weight,
        conv_bias,
        dt_bias,
        a_log,
    )
    x_part, b_part, c_part, step_size, cumulated = prepared
    (state_piece, decay), state_back = jax.vjp(local_state, x_part, b_part, step_size, cumulated)
    upstream = cotangent.astype(jnp.float32)
    state_in = pass_states(decay, state_piece)
    result, output_back = jax.vjp(
        outputs, x_part, b_part, c_part, step_size, cumulated, state_in, d_skip
    )
    grad_x, grad_b, grad_c, grad_step, grad_cum, adjoint_in, grad_skip = output_back(upstream)
    adjoint_out = pass_adjoints(decay, adjoint_in)
    decay_grad = jnp.sum(adjoint_out * state_in, axis=(1, 2))
    state_x, state_b, state_step, state_cum = state_back((adjoint_out, decay_grad))
    pieces = prep_back(
        (grad_x + state_x, grad_b + state_b, grad_c, grad_step + state_step, grad_cum + state_cum)
    )
    grad_block, grad_edge, grad_raw, grad_weight, grad_bias, grad_dtbias, grad_alog = pieces
    from_next = shifted(grad_edge, "seq", -1)
    grad_block = grad_block.at[row_count - margin :].add(from_next)
    totals = lax.psum((grad_weight, grad_bias, grad_dtbias, grad_alog, grad_skip), "seq")
    return (
        grad_block.astype(jnp.bfloat16),
        grad_raw,
        totals[0],
        totals[1],
        totals[2],
        totals[3],
        totals[4],
    )


def solution(mesh):
    placed = (
        P(("groups", "seq"), None),
        P(None, ("groups", "seq")),
        P(("groups", "seq"), None),
        P(),
        P(),
        P(),
        P(),
        P(),
    )
    return jax.shard_map(
        local,
        mesh=mesh,
        in_specs=placed,
        out_specs=(
            P(("groups", "seq"), None),
            P(None, ("groups", "seq")),
            P("groups", None),
            P("groups"),
            P("groups"),
            P("groups"),
            P("groups"),
        ),
        check_vma=False,
    )
```

profile of v0, /device:TPU:0, one launch (start us, length us, event | category | flops | bytes accessed | tf_op | source)
XLA Modules:
  0.0 587.8 jit_solution(7906634695144241195)
XLA Ops:
  8.6 2.9 collective-permute-start
  17.0 1.8 copy.213
  20.3 3.2 reduce_window_sum.22
  26.0 3.8 multiply_convert_fusion.5
  34.0 1.9 broadcast.156.clone.2
  35.8 1.9 broadcast.159.clone
  39.1 18.8 %while.151 = (s32[]{:T(128)}, f32[40]{0:T(128)S(1)}, f32[40,64,32]{1,2,0:T(8,128)S(1)}, f32[4,40,128]{2,1,0:T(8,128)S(1)}, f32[4,128,40,1]{1,2,3,0:T(8,128)}, /*...) while((s32[]{:T(128)}, f32[40]{0:T(128)S(1)}, ...), condition=%wide.region_2.3_spmd.clone, body=%wide.region_1.2_spmd.clone.sunk | while | flops 126835792 | bytes 7034777 | solution.py:162
  58.8 3.2 convert.9
  63.4 33.7 %all-reduce.15 = bf16[640]{0:T(1024)(128)(2,1)S(1)} all-reduce(bf16[640]{0:T(1024)(128)(2,1)S(1)} %dynamic-update-slice.3), channel_id=2, replica_groups=mesh['groups'=2,'seq'=16] {'seq'}, use_global_device_ids=true, to_apply=%add.15 | all-reduce | flops 640 | bytes 2560
  98.0 19.0 %all-gather.6.cloned.1.call-done = bf16[640,64,32]{1,2,0:T(8,128)(2,1)} async-done(((bf16[40,64,32]{1,2,0:T(8,128)(2,1)}), bf16[640,64,32]{1,2,0:T(8,128)(2,1)}) %all-gather.6.cloned.1.call-update) | async-done | bytes 2621456 | tf_op jit(solution)/shard_map/all_gather | solution.py:15
  117.5 1.9 broadcast.156
  121.2 1.8 broadcast.159
  126.5 35.8 %while.149 = (s32[]{:T(128)}, f32[40,64,32]{1,2,0:T(8,128)S(1)}, f32[4,40,64,32]{2,3,1,0:T(8,128)}, f32[4,128,64]{1,2,0:T(8,128)S(1)}, f32[4,40,128]{1,2,0:T(8,1...) while((s32[]{:T(128)}, f32[40,64,32]{1,2,0:T(8,128)S(1)}, ...), condition=%wide.region_6.7_spmd, body=%wide.region_5.6_spmd.sunk | while | flops 252509184 | bytes 8542841 | solution.py:146
  166.2 153.4 %while.152 = (s32[]{:T(128)}, f32[40]{0:T(128)}, f32[40,64,32]{1,2,0:T(8,128)S(1)}, bf16[4,128,1280]{1,2,0:T(8,128)(2,1)}, bf16[4,128,64]{1,2,0:T(8,128)(2,1)}, ...) while((s32[]{:T(128)}, f32[40]{0:T(128)}, ...), condition=%wide.region_18.19_spmd.clone, body=%wide.region_7.18_spmd.clone.sunk | while | flops 611158016 | bytes 27024728 | solution.py:146
  170.4 3.1 fusion.243
  176.8 2.0 fusion.239
  180.1 2.6 fusion.240
  182.7 2.3 constant_dynamic-slice_fusion.25
  193.9 2.4 fusion.245
  197.9 2.8 fusion.242
  208.8 3.1 fusion.243
  215.2 2.0 fusion.239
  218.5 2.6 fusion.240
  221.1 2.3 constant_dynamic-slice_fusion.25
  232.3 2.4 fusion.245
  236.2 2.8 fusion.242
  247.2 3.1 fusion.243
  253.5 2.0 fusion.239
  256.9 2.6 fusion.240
  259.4 2.3 constant_dynamic-slice_fusion.25
  270.7 2.4 fusion.245
  274.6 2.8 fusion.242
  285.5 3.1 fusion.243
  291.9 2.0 fusion.239
  295.2 2.6 fusion.240
  297.8 2.3 constant_dynamic-slice_fusion.25
  309.0 2.4 fusion.245
  313.0 2.8 fusion.242
  322.8 77.7 %all-gather.8.cloned.1.call-done = bf16[640,64,32]{1,2,0:T(8,128)(2,1)} async-done(((bf16[40,64,32]{1,2,0:T(8,128)(2,1)}), bf16[640,64,32]{1,2,0:T(8,128)(2,1)}) %all-gather.8.cloned.1.call-update) | async-done | bytes 2621456 | tf_op jit(solution)/shard_map/all_gather | solution.py:35
  400.4 37.9 %while.153 = (s32[]{:T(128)}, f32[40,64,32]{2,1,0:T(8,128)S(1)}, s32[]{:T(128)}, bf16[16,40]{1,0:T(8,128)(2,1)}, bf16[16,40,64,32]{2,3,1,0:T(8,128)(2,1)}, /*index=5*/s32[]{:T(128)}, s32[]{:T(128)}, s32[]{:T(128)}, s32[]{:T(128)}) while((s32[]{:T(128)}, f32[40,64,32]{2,1,0:T(8,128)S(1)}, s32[]{:T(128)}, ...), condition=%wide.region_20.21_spmd.clone, body=%wide.region_19.20_spmd.clone.sunk | while | flops 409648 | bytes 1475127 | solution.py:53
  440.4 36.4 %while.150 = (s32[]{:T(128)}, f32[40]{0:T(128)S(1)}, f32[40,64,32]{1,0,2:T(8,128)S(1)}, bf16[4,128,1280]{1,2,0:T(8,128)(2,1)S(1)}, bf16[4,128,64]{1,2,0:T(8,128)...) while((s32[]{:T(128)}, f32[40]{0:T(128)S(1)}, ...), condition=%wide.region_26.27_spmd, body=%wide.region_22.26_spmd.sunk | while | flops 252608608 | bytes 8530497 | solution.py:162
  477.9 3.3 add.217
  481.1 2.4 copy.207
  483.6 5.1 multiply_reduce_fusion.2
  492.9 2.1 pad_add_fusion
  506.5 5.7 reduce_window_sum.23
  515.2 2.8 split.8
  518.0 60.7 %all-reduce.16 = (f32[4,1408]{1,0:T(4,128)}, f32[1408]{0:T(1024)}, f32[40]{0:T(128)}, f32[40]{0:T(128)}, f32[40]{0:T(128)}) all-reduce(f32[4,1408]{1,0:T(4,128)S(1)} %pad_add_fusion.2, f32[1408]{0:T(1024)S(1)} %get-tuple-element.1915, f32[40]{0:T(128)S(1)} %get-tuple-element.2106, ...), channel_id=1, replica_groups=mesh['groups'=2,'seq'=16] {'seq'}, use_global_device_ids=true, to_apply=%region_32.33 | all-reduce | flops 7160 | bytes 57280 | tf_op jit(solution)/shard_map/psum | solution.py:213
  (688 shorter events, 275.0 us)
Async XLA Ops:
  7.2 109.8 %all-gather.6.cloned.1.call-start = ((), (), s32[]{:S(2)}) async-start(), calls=%async_computation | async-start | bytes 5570560 | tf_op jit(solution)/shard_map/all_gather | solution.py:15
  8.6 16.7 %collective-permute-start = (bf16[3,1408]{1,0:T(4,128)(2,1)}, bf16[3,1408]{1,0:T(4,128)(2,1)}, u32[]{:S(2)}, u32[]{:S(2)}) collective-permute-start(bf16[3,1408]{1,0:T(4,128)(2,1)} %slice.64), channel_id=1, source_target_pairs={{0,1},{1,2},{2,3},{3,4},{4,5},{5,6},{6,7},{7,8},{8,9},{9,10},{10,1... | collective-permute-start | bytes 25352 | tf_op jit(solution)/shard_map/ppermute | solution.py:59
  15.4 10.6 %copy-start.36 = (f32[1408]{0:T(1024)}, f32[1408]{0:T(1024)S(1)}, u32[]{:S(2)}) copy-start(f32[1408]{0:T(1024)S(1)} %get-tuple-element.1918) | copy-start | bytes 16900
  16.9 12.8 %copy-start.7 = (f32[512,1408]{1,0:T(8,128)}, f32[512,1408]{1,0:T(8,128)S(1)}, u32[]{:S(2)}) copy-start(f32[512,1408]{1,0:T(8,128)S(1)} %convert_element_type.255) | copy-start | bytes 8650756
  57.9 39.4 %copy-start.19 = (bf16[512,64]{1,0:T(8,128)(2,1)S(1)}, bf16[512,64]{1,0:T(8,128)(2,1)}, u32[]{:S(2)}) copy-start(bf16[512,64]{1,0:T(8,128)(2,1)} %get-tuple-element.2160) | copy-start | bytes 196612
  58.7 341.8 %all-gather.8.cloned.1.call-start = ((), (), s32[]{:S(2)}) async-start(), calls=%async_computation.1 | async-start | bytes 5570560 | tf_op jit(solution)/shard_map/all_gather | solution.py:35
  119.4 7.1 %copy-start.18 = (bf16[4,128,64]{1,2,0:T(8,128)(2,1)S(1)}, bf16[4,128,64]{1,2,0:T(8,128)(2,1)}, u32[]{:S(2)}) copy-start(bf16[4,128,64]{1,2,0:T(8,128)(2,1)} %copy.180) | copy-start | bytes 196612
  119.4 7.1 %copy-start.26 = (bf16[4,128,64]{1,2,0:T(8,128)(2,1)S(1)}, bf16[4,128,64]{1,2,0:T(8,128)(2,1)}, u32[]{:S(2)}) copy-start(bf16[4,128,64]{1,2,0:T(8,128)(2,1)} %copy.187) | copy-start | bytes 196612
  166.2 7.4 %copy-start.27 = (f32[4,128,64]{1,2,0:T(8,128)}, f32[4,128,64]{1,2,0:T(8,128)S(1)}, u32[]{:S(2)}) copy-start(f32[4,128,64]{1,2,0:T(8,128)S(1)} %get-tuple-element.3035) | copy-start | bytes 393220 | tf_op jit(solution)/shard_map/transpose(jvp())/while
  191.2 9.6 %copy-start.13 = (bf16[128,64]{1,0:T(8,128)(2,1)S(1)}, bf16[128,64]{1,0:T(8,128)(2,1)}, u32[]{:S(2)}) copy-start(bf16[128,64]{1,0:T(8,128)(2,1)} %copy-done.12) | copy-start | bytes 49156 | tf_op jit(solution)/shard_map/transpose(jvp())/while
  191.2 9.6 %copy-start.16 = (bf16[128,128]{1,0:T(8,128)(2,1)S(1)}, bf16[128,128]{1,0:T(8,128)(2,1)}, u32[]{:S(2)}) copy-start(bf16[128,128]{1,0:T(8,128)(2,1)} %get-tuple-element.2807) | copy-start | bytes 98308 | tf_op jit(solution)/shard_map/transpose(jvp())/while
  191.2 10.4 %copy-start.6 = (bf16[128,40,32]{0,1,2:T(8,128)(2,1)S(1)}, bf16[128,40,32]{0,1,2:T(8,128)(2,1)}, u32[]{:S(2)}) copy-start(bf16[128,40,32]{0,1,2:T(8,128)(2,1)} %get-tuple-element.2804) | copy-start | bytes 983044 | tf_op jit(solution)/shard_map/transpose(jvp())/while
  192.9 8.7 %copy-start.44 = (f32[1,40,1]{1,2,0:T(1,128)S(1)}, f32[1,40,1]{1,2,0:T(1,128)}, u32[]{:S(2)}) copy-start(f32[1,40,1]{1,2,0:T(1,128)} %get-tuple-element.3043) | copy-start | bytes 484 | tf_op jit(solution)/shard_map/transpose(jvp())/while
  193.9 8.8 %copy-start.52 = (f32[4,40,1,1]{1,3,2,0:T(1,128)S(1)}, f32[4,40,1,1]{1,3,2,0:T(1,128)}, u32[]{:S(2)}) copy-start(f32[4,40,1,1]{1,3,2,0:T(1,128)} %copy-done.51) | copy-start | bytes 1924 | tf_op jit(solution)/shard_map/transpose(jvp())/while
  193.9 8.8 %copy-start.28 = (f32[4,128,64]{1,2,0:T(8,128)S(1)}, f32[4,128,64]{1,2,0:T(8,128)}, u32[]{:S(2)}) copy-start(f32[4,128,64]{1,2,0:T(8,128)} %copy-done.27) | copy-start | bytes 393220 | tf_op jit(solution)/shard_map/transpose(jvp())/while
  197.9 6.1 %copy-start.41 = (f32[40]{0:T(128)S(1)}, f32[40]{0:T(128)}, u32[]{:S(2)}) copy-start(f32[40]{0:T(128)} %get-tuple-element.2993) | copy-start | bytes 484 | tf_op jit(solution)/shard_map/transpose(jvp())/while
  197.9 6.7 %copy-start.48 = (f32[4,40]{1,0:T(4,128)S(1)}, f32[4,40]{1,0:T(4,128)}, u32[]{:S(2)}) copy-start(f32[4,40]{1,0:T(4,128)} %copy-done.47) | copy-start | bytes 1924 | tf_op jit(solution)/shard_map/transpose(jvp())/while
  204.6 7.4 %copy-start.27 = (f32[4,128,64]{1,2,0:T(8,128)}, f32[4,128,64]{1,2,0:T(8,128)S(1)}, u32[]{:S(2)}) copy-start(f32[4,128,64]{1,2,0:T(8,128)S(1)} %get-tuple-element.3035) | copy-start | bytes 393220 | tf_op jit(solution)/shard_map/transpose(jvp())/while
  229.5 9.6 %copy-start.13 = (bf16[128,64]{1,0:T(8,128)(2,1)S(1)}, bf16[128,64]{1,0:T(8,128)(2,1)}, u32[]{:S(2)}) copy-start(bf16[128,64]{1,0:T(8,128)(2,1)} %copy-done.12) | copy-start | bytes 49156 | tf_op jit(solution)/shard_map/transpose(jvp())/while
  229.5 9.6 %copy-start.16 = (bf16[128,128]{1,0:T(8,128)(2,1)S(1)}, bf16[128,128]{1,0:T(8,128)(2,1)}, u32[]{:S(2)}) copy-start(bf16[128,128]{1,0:T(8,128)(2,1)} %get-tuple-element.2807) | copy-start | bytes 98308 | tf_op jit(solution)/shard_map/transpose(jvp())/while
  229.5 10.4 %copy-start.6 = (bf16[128,40,32]{0,1,2:T(8,128)(2,1)S(1)}, bf16[128,40,32]{0,1,2:T(8,128)(2,1)}, u32[]{:S(2)}) copy-start(bf16[128,40,32]{0,1,2:T(8,128)(2,1)} %get-tuple-element.2804) | copy-start | bytes 983044 | tf_op jit(solution)/shard_map/transpose(jvp())/while
  231.3 8.7 %copy-start.44 = (f32[1,40,1]{1,2,0:T(1,128)S(1)}, f32[1,40,1]{1,2,0:T(1,128)}, u32[]{:S(2)}) copy-start(f32[1,40,1]{1,2,0:T(1,128)} %get-tuple-element.3043) | copy-start | bytes 484 | tf_op jit(solution)/shard_map/transpose(jvp())/while
  232.3 8.8 %copy-start.52 = (f32[4,40,1,1]{1,3,2,0:T(1,128)S(1)}, f32[4,40,1,1]{1,3,2,0:T(1,128)}, u32[]{:S(2)}) copy-start(f32[4,40,1,1]{1,3,2,0:T(1,128)} %copy-done.51) | copy-start | bytes 1924 | tf_op jit(solution)/shard_map/transpose(jvp())/while
  232.3 8.8 %copy-start.28 = (f32[4,128,64]{1,2,0:T(8,128)S(1)}, f32[4,128,64]{1,2,0:T(8,128)}, u32[]{:S(2)}) copy-start(f32[4,128,64]{1,2,0:T(8,128)} %copy-done.27) | copy-start | bytes 393220 | tf_op jit(solution)/shard_map/transpose(jvp())/while
  236.2 6.7 %copy-start.48 = (f32[4,40]{1,0:T(4,128)S(1)}, f32[4,40]{1,0:T(4,128)}, u32[]{:S(2)}) copy-start(f32[4,40]{1,0:T(4,128)} %copy-done.47) | copy-start | bytes 1924 | tf_op jit(solution)/shard_map/transpose(jvp())/while
  242.9 7.4 %copy-start.27 = (f32[4,128,64]{1,2,0:T(8,128)}, f32[4,128,64]{1,2,0:T(8,128)S(1)}, u32[]{:S(2)}) copy-start(f32[4,128,64]{1,2,0:T(8,128)S(1)} %get-tuple-element.3035) | copy-start | bytes 393220 | tf_op jit(solution)/shard_map/transpose(jvp())/while
  267.9 9.6 %copy-start.13 = (bf16[128,64]{1,0:T(8,128)(2,1)S(1)}, bf16[128,64]{1,0:T(8,128)(2,1)}, u32[]{:S(2)}) copy-start(bf16[128,64]{1,0:T(8,128)(2,1)} %copy-done.12) | copy-start | bytes 49156 | tf_op jit(solution)/shard_map/transpose(jvp())/while
  267.9 9.6 %copy-start.16 = (bf16[128,128]{1,0:T(8,128)(2,1)S(1)}, bf16[128,128]{1,0:T(8,128)(2,1)}, u32[]{:S(2)}) copy-start(bf16[128,128]{1,0:T(8,128)(2,1)} %get-tuple-element.2807) | copy-start | bytes 98308 | tf_op jit(solution)/shard_map/transpose(jvp())/while
  267.9 10.4 %copy-start.6 = (bf16[128,40,32]{0,1,2:T(8,128)(2,1)S(1)}, bf16[128,40,32]{0,1,2:T(8,128)(2,1)}, u32[]{:S(2)}) copy-start(bf16[128,40,32]{0,1,2:T(8,128)(2,1)} %get-tuple-element.2804) | copy-start | bytes 983044 | tf_op jit(solution)/shard_map/transpose(jvp())/while
  269.6 8.7 %copy-start.44 = (f32[1,40,1]{1,2,0:T(1,128)S(1)}, f32[1,40,1]{1,2,0:T(1,128)}, u32[]{:S(2)}) copy-start(f32[1,40,1]{1,2,0:T(1,128)} %get-tuple-element.3043) | copy-start | bytes 484 | tf_op jit(solution)/shard_map/transpose(jvp())/while
  270.6 8.8 %copy-start.52 = (f32[4,40,1,1]{1,3,2,0:T(1,128)S(1)}, f32[4,40,1,1]{1,3,2,0:T(1,128)}, u32[]{:S(2)}) copy-start(f32[4,40,1,1]{1,3,2,0:T(1,128)} %copy-done.51) | copy-start | bytes 1924 | tf_op jit(solution)/shard_map/transpose(jvp())/while
  270.6 8.8 %copy-start.28 = (f32[4,128,64]{1,2,0:T(8,128)S(1)}, f32[4,128,64]{1,2,0:T(8,128)}, u32[]{:S(2)}) copy-start(f32[4,128,64]{1,2,0:T(8,128)} %copy-done.27) | copy-start | bytes 393220 | tf_op jit(solution)/shard_map/transpose(jvp())/while
  274.6 6.7 %copy-start.48 = (f32[4,40]{1,0:T(4,128)S(1)}, f32[4,40]{1,0:T(4,128)}, u32[]{:S(2)}) copy-start(f32[4,40]{1,0:T(4,128)} %copy-done.47) | copy-start | bytes 1924 | tf_op jit(solution)/shard_map/transpose(jvp())/while
  281.3 7.4 %copy-start.27 = (f32[4,128,64]{1,2,0:T(8,128)}, f32[4,128,64]{1,2,0:T(8,128)S(1)}, u32[]{:S(2)}) copy-start(f32[4,128,64]{1,2,0:T(8,128)S(1)} %get-tuple-element.3035) | copy-start | bytes 393220 | tf_op jit(solution)/shard_map/transpose(jvp())/while
  306.2 9.6 %copy-start.13 = (bf16[128,64]{1,0:T(8,128)(2,1)S(1)}, bf16[128,64]{1,0:T(8,128)(2,1)}, u32[]{:S(2)}) copy-start(bf16[128,64]{1,0:T(8,128)(2,1)} %copy-done.12) | copy-start | bytes 49156 | tf_op jit(solution)/shard_map/transpose(jvp())/while
  306.2 9.6 %copy-start.16 = (bf16[128,128]{1,0:T(8,128)(2,1)S(1)}, bf16[128,128]{1,0:T(8,128)(2,1)}, u32[]{:S(2)}) copy-start(bf16[128,128]{1,0:T(8,128)(2,1)} %get-tuple-element.2807) | copy-start | bytes 98308 | tf_op jit(solution)/shard_map/transpose(jvp())/while
  306.3 10.4 %copy-start.6 = (bf16[128,40,32]{0,1,2:T(8,128)(2,1)S(1)}, bf16[128,40,32]{0,1,2:T(8,128)(2,1)}, u32[]{:S(2)}) copy-start(bf16[128,40,32]{0,1,2:T(8,128)(2,1)} %get-tuple-element.2804) | copy-start | bytes 983044 | tf_op jit(solution)/shard_map/transpose(jvp())/while
  308.0 8.7 %copy-start.44 = (f32[1,40,1]{1,2,0:T(1,128)S(1)}, f32[1,40,1]{1,2,0:T(1,128)}, u32[]{:S(2)}) copy-start(f32[1,40,1]{1,2,0:T(1,128)} %get-tuple-element.3043) | copy-start | bytes 484 | tf_op jit(solution)/shard_map/transpose(jvp())/while
  309.0 8.8 %copy-start.52 = (f32[4,40,1,1]{1,3,2,0:T(1,128)S(1)}, f32[4,40,1,1]{1,3,2,0:T(1,128)}, u32[]{:S(2)}) copy-start(f32[4,40,1,1]{1,3,2,0:T(1,128)} %copy-done.51) | copy-start | bytes 1924 | tf_op jit(solution)/shard_map/transpose(jvp())/while
  309.0 8.8 %copy-start.28 = (f32[4,128,64]{1,2,0:T(8,128)S(1)}, f32[4,128,64]{1,2,0:T(8,128)}, u32[]{:S(2)}) copy-start(f32[4,128,64]{1,2,0:T(8,128)} %copy-done.27) | copy-start | bytes 393220 | tf_op jit(solution)/shard_map/transpose(jvp())/while
  313.0 6.1 %copy-start.41 = (f32[40]{0:T(128)S(1)}, f32[40]{0:T(128)}, u32[]{:S(2)}) copy-start(f32[40]{0:T(128)} %get-tuple-element.2993) | copy-start | bytes 484 | tf_op jit(solution)/shard_map/transpose(jvp())/while
  313.0 6.7 %copy-start.48 = (f32[4,40]{1,0:T(4,128)S(1)}, f32[4,40]{1,0:T(4,128)}, u32[]{:S(2)}) copy-start(f32[4,40]{1,0:T(4,128)} %copy-done.47) | copy-start | bytes 1924 | tf_op jit(solution)/shard_map/transpose(jvp())/while
  440.3 37.0 %copy-start.33 = (bf16[4,128,64]{1,2,0:T(8,128)(2,1)S(1)}, bf16[4,128,64]{1,2,0:T(8,128)(2,1)}, u32[]{:S(2)}) copy-start(bf16[4,128,64]{1,2,0:T(8,128)(2,1)} %get-tuple-element.1383) | copy-start | bytes 196612
  492.9 6.2 %copy-start.22 = (f32[4,40,128]{1,2,0:T(8,128)S(1)}, f32[4,40,128]{1,2,0:T(8,128)}, u32[]{:S(2)}) copy-start(f32[4,40,128]{1,2,0:T(8,128)} %get-tuple-element.1400) | copy-start | bytes 245764
  492.9 10.6 %copy-start.21 = (f32[4,40,128]{1,2,0:T(8,128)S(1)}, f32[4,40,128]{1,2,0:T(8,128)}, u32[]{:S(2)}) copy-start(f32[4,40,128]{1,2,0:T(8,128)} %get-tuple-element.1398) | copy-start | bytes 245764
  494.9 17.3 %copy-start.30 = (f32[40,512]{1,0:T(8,128)S(1)}, f32[40,512]{1,0:T(8,128)}, u32[]{:S(2)}) copy-start(f32[40,512]{1,0:T(8,128)} %param.23) | copy-start | bytes 245764
  495.5 18.3 %copy-start.40 = (f32[1,1408]{1,0:T(1,128)S(1)}, f32[1,1408]{1,0:T(1,128)}, u32[]{:S(2)}) copy-start(f32[1,1408]{1,0:T(1,128)} %reshape.488) | copy-start | bytes 16900
  505.2 73.5 %collective-permute-start.1 = (f32[3,1408]{1,0:T(4,128)S(1)}, f32[3,1408]{1,0:T(4,128)S(1)}, u32[]{:S(2)}, u32[]{:S(2)}) collective-permute-start(f32[3,1408]{1,0:T(4,128)S(1)} %pad_add_fusion.1), channel_id=1, source_target_pairs={{1,0},{2,1},{3,2},{4,3},{5,4},{6,5},{7,6},{8,7},{9,8},{10,9},{11,1... | collective-permute-start | bytes 50696 | tf_op jit(solution)/shard_map/ppermute | solution.py:59
  (56 other events, 202.8 us)
Sparse Core Ops, SparseCore 0:
  58.8 58.1 all-gather.5
  320.6 79.8 all-gather.7
where the time goes:
time: 595 us; the launch traced here: 588 us
  local copies, waits for them, and re-layouts  158 us (27%)
  other arithmetic  130 us (22%)
  waiting for transfers between devices  96.7 us (16%)
  blocking collectives  94.5 us (16%)
  matrix products  87.2 us (15%)
  between operations  15.2 us (3%)
    all_gather x1, waiting for transfers between devices, carried_in(): lax.all_gather(part.astype(kind), axis)  77.7 us
    psum x1, blocking collectives, local(): lax.psum((grad_weight, grad_bias, grad_dtbias, grad_alog, grad_skip), 'seq')  60.7 us
    dot_general x24, matrix products, block_state(): jnp.einsum('tn,thp->hnp', b_part.astype(jnp.float32), scaled, precision=l...  40.3 us
    unnamed x1, blocking collectives  33.7 us
    dynamic_slice x24, local copies, waits for them, and re-layouts, outputs(): lax.scan(outputs_advance, state_in, to_blocks(x_part, b_part, c_part, ste...  29.4 us
    dynamic_update_slice x32, other arithmetic, local_state(): lax.scan(local_advance, start, (blocked[0], blocked[1], blocked[3], block...  28.8 us
    dynamic_slice x32, local copies, waits for them, and re-layouts, hop(): part[at].astype(own.dtype)  21.1 us
    dot_general x12, matrix products, block_outputs(): jnp.einsum('tn,hnp->thp', c_part.astype(jnp.float32), state_in, precision...  20.2 us
  transfers between devices with their start and end apart: 4, of which 2 were waited for; matrix products, arithmetic and copies ran while one was open for 6% of the time, Pallas kernels for 0%

commit v1 on v0

v1 whole, which is shorter than its diff:
```python
import functools

import jax
import jax.numpy as jnp
from jax import lax
from jax.experimental import pallas as pl
from jax.experimental.pallas import tpu as pltpu
from jax.sharding import PartitionSpec as P

HEADS = 40
HEAD_DIM = 32
STATE = 64
BLOCK = 128
INNER = HEADS * HEAD_DIM
CONV = INNER + 2 * STATE
MEMBERS = 4
SLICE = STATE // MEMBERS
F32 = jnp.float32
BF16 = jnp.bfloat16
EXACT = lax.Precision.HIGHEST


def mm(a, b, ca, cb, precision=None):
    return lax.dot_general(
        a, b, (((ca,), (cb,)), ((), ())), precision=precision, preferred_element_type=F32
    )


def iota(shape, dim):
    return lax.broadcasted_iota(jnp.int32, shape, dim)


def split(v):
    high = v.astype(BF16)
    return high, (v - high.astype(F32)).astype(BF16)


def column(row):
    width = row.shape[1]
    eye = iota((width, width), 0) == iota((width, width), 1)
    return jnp.sum(jnp.where(eye, jnp.broadcast_to(row, (width, width)), 0.0), axis=1, keepdims=True)


def kernel(
    n,
    x_ref, dt_ref, cot_ref, w_ref, bias_ref, dtb_ref, alog_ref, skip_ref,
    gx_ref, gdt_ref, gw_ref, gbias_ref, gdtb_ref, galog_ref, gskip_ref,
    xs, edge, act, dsil, xt, gt, fx, u_ref, v_ref, ds_ref, piece, back, fall_ref,
    step_ref, sig_ref, msg, r1, msg2, r2, msg3, r3, cin, ain, dz, dz_edge, prm, p1, p2s, p2,
    edge_sem, s1, q1, s2, q2, s3, q3, dz_sem, s4, q4, s5, q5,
):
    rows = x_ref.shape[0]
    blocks = rows // BLOCK
    groups = n // MEMBERS
    me = lax.axis_index("seq")
    g = me // MEMBERS
    m = me % MEMBERS
    base = g * MEMBERS

    def remote(src, dst, send, recv, to):
        return pltpu.make_async_remote_copy(
            src_ref=src, dst_ref=dst, send_sem=send, recv_sem=recv,
            device_id={"seq": to}, device_id_type=pl.DeviceIdType.MESH,
        )

    barrier = pltpu.get_barrier_semaphore()

    def greet(k, carry):
        pl.semaphore_signal(
            barrier, inc=1, device_id={"seq": (me + k) % n}, device_id_type=pl.DeviceIdType.MESH
        )
        return carry

    lax.fori_loop(1, n, greet, 0)
    pl.semaphore_wait(barrier, n - 1)

    def edge_copy():
        return remote(
            x_ref.at[pl.ds(rows - 16, 16)], edge, edge_sem.at[0], edge_sem.at[1],
            jnp.minimum(me + 1, n - 1),
        )

    @pl.when(me < n - 1)
    def _():
        edge_copy().start()

    alog = column(alog_ref[...])
    neg_a = -jnp.exp(alog)
    raw = dt_ref[...] + column(dtb_ref[...])
    step = jnp.maximum(raw, 0.0) + jnp.log1p(jnp.exp(-jnp.abs(raw)))
    step_ref[...] = step
    sig_ref[...] = 1.0 / (1.0 + jnp.exp(-raw))
    later = iota((BLOCK, BLOCK), 0) <= iota((BLOCK, BLOCK), 1)
    tri = jnp.where(later, 1.0, 0.0)
    causal = iota((BLOCK, BLOCK), 0) >= iota((BLOCK, BLOCK), 1)
    head_row = iota((2 * HEADS, INNER), 0)
    head_row = jnp.where(head_row >= HEADS, head_row - HEADS, head_row)
    spread2 = jnp.where((iota((2 * HEADS, INNER), 1) >> 5) == head_row, 1.0, 0.0).astype(BF16)
    spread_f = jnp.where((iota((HEADS, INNER), 1) >> 5) == iota((HEADS, INNER), 0), 1.0, 0.0)
    spread1 = spread_f.astype(BF16)

    def expand(v):
        high = v.astype(BF16).astype(F32)
        both = jnp.concatenate([high, v - high], axis=0).astype(BF16)
        return mm(both, spread2, 0, 0)

    def per_head(v):
        high, low = split(v)
        return mm(spread1, high, 1, 1) + mm(spread1, low, 1, 1)

    xs[pl.ds(8, rows)] = x_ref[...].astype(F32)
    for b in list(range(1, blocks)) + [0]:
        t0 = b * BLOCK
        if b == 0:
            xs[pl.ds(0, 8)] = jnp.zeros((8, CONV), F32)

            @pl.when(me > 0)
            def _():
                edge_copy().wait_recv()
                xs[pl.ds(0, 8)] = edge[...].astype(F32)[8:16]

        for j in range(CONV // 128):
            lanes = pl.ds(j * 128, 128)
            z = jnp.broadcast_to(bias_ref[:, lanes], (BLOCK, 128))
            for k in range(4):
                z = z + w_ref[pl.ds(k, 1), lanes] * xs[pl.ds(t0 + 5 + k, BLOCK), lanes]
            s = 1.0 / (1.0 + jnp.exp(-z))
            act[pl.ds(t0, BLOCK), lanes] = (z * s).astype(BF16)
            dsil[pl.ds(t0, BLOCK), lanes] = s * (1.0 + z * (1.0 - s))

        rate = neg_a * step_ref[:, pl.ds(t0, BLOCK)]
        cum = mm(rate, tri, 1, 0, EXACT)
        grow = expand(jnp.exp(cum))
        fade = expand(jnp.exp(-cum) * step_ref[:, pl.ds(t0, BLOCK)])
        fx[pl.ds(t0, BLOCK)] = fade
        fall_ref[pl.ds(b * 8, 8)] = jnp.broadcast_to(grow[BLOCK - 1 : BLOCK], (8, INNER))
        xtb = (fade * act[pl.ds(t0, BLOCK), pl.ds(0, INNER)].astype(F32)).astype(BF16)
        gtb = (grow * cot_ref[pl.ds(t0, BLOCK)].astype(F32)).astype(BF16)
        xt[pl.ds(t0, BLOCK)] = xtb
        gt[pl.ds(t0, BLOCK)] = gtb
        bc = act[pl.ds(t0, BLOCK), pl.ds(INNER, 2 * STATE)]
        piece[pl.ds(b * STATE, STATE)] = mm(bc, xtb, 0, 0)[:STATE]
        back[pl.ds(b * STATE, STATE)] = mm(bc, gtb, 0, 0)[STATE:]

    state = jnp.zeros((STATE, INNER), F32)
    adj = jnp.zeros((STATE, INNER), F32)
    decay = jnp.ones((1, INNER), F32)
    for b in range(blocks):
        fall = fall_ref[pl.ds(b * 8, 1)]
        state = fall * (state + piece[pl.ds(b * STATE, STATE)])
        decay = decay * fall
    for b in reversed(range(blocks)):
        adj = fall_ref[pl.ds(b * 8, 1)] * adj + back[pl.ds(b * STATE, STATE)]

    def pack_decay(d):
        d16 = jnp.broadcast_to(d, (SLICE, INNER))
        high = d16.astype(BF16).astype(F32)
        rest = d16 - high
        mid = rest.astype(BF16).astype(F32)
        low = rest - mid
        at = iota((SLICE, INNER), 0)
        return jnp.where(at == 0, high, jnp.where(at == 1, mid, jnp.where(at == 2, low, 0.0))).astype(BF16)

    def unpack_decay(d):
        return jnp.sum(d.astype(F32), axis=0, keepdims=True)

    packed = pack_decay(decay)
    for j in range(MEMBERS):
        msg[j, pl.ds(0, SLICE)] = state[j * SLICE : (j + 1) * SLICE].astype(BF16)
        msg[j, pl.ds(SLICE, SLICE)] = packed
        msg[j, pl.ds(2 * SLICE, SLICE)] = adj[j * SLICE : (j + 1) * SLICE].astype(BF16)

    def round1(off):
        to = (m + off) % MEMBERS
        return remote(msg.at[to], r1.at[m], s1.at[off], q1.at[off], base + to)

    def round1_in(off):
        frm = (m + MEMBERS - off) % MEMBERS
        return remote(msg.at[frm], r1.at[frm], s1.at[off], q1.at[off], base + frm)

    for off in range(1, MEMBERS):
        round1(off).start()
    r1[m] = msg[m]

    def intra(b):
        t0 = b * BLOCK
        bc = act[pl.ds(t0, BLOCK), pl.ds(INNER, 2 * STATE)]
        xtb, gtb = xt[pl.ds(t0, BLOCK)], gt[pl.ds(t0, BLOCK)]
        scores = mm(bc[:, STATE:], bc[:, :STATE], 1, 1)
        smb = jnp.where(causal, scores, 0.0).astype(BF16)
        u_ref[pl.ds(t0, BLOCK)] = mm(smb, xtb, 1, 0)
        v_ref[pl.ds(t0, BLOCK)] = mm(smb, gtb, 0, 0)
        ds_ref[pl.ds(t0, BLOCK)] = jnp.where(causal, mm(gtb, xtb, 1, 1), 0.0).astype(BF16)

    half = blocks // 2
    for b in range(half):
        intra(b)

    for off in range(1, MEMBERS):
        round1_in(off).wait_recv()
    decays = [unpack_decay(r1[i, pl.ds(SLICE, SLICE)]) for i in range(MEMBERS)]
    gs = jnp.zeros((SLICE, INNER), F32)
    ga = jnp.zeros((SLICE, INNER), F32)
    gd = jnp.ones((1, INNER), F32)
    for i in range(MEMBERS):
        gs = decays[i] * gs + r1[i, pl.ds(0, SLICE)].astype(F32)
        gd = gd * decays[i]
    for i in reversed(range(MEMBERS)):
        ga = decays[i] * ga + r1[i, pl.ds(2 * SLICE, SLICE)].astype(F32)
    msg2[pl.ds(0, SLICE)] = gs.astype(BF16)
    msg2[pl.ds(SLICE, SLICE)] = pack_decay(gd)
    msg2[pl.ds(2 * SLICE, SLICE)] = ga.astype(BF16)

    def round2(off):
        to = (g + off) % groups
        part = pl.ds(pl.multiple_of(jnp.where(to > g, 0, SLICE), SLICE), 2 * SLICE)
        return remote(
            msg2.at[part], r2.at[g, part], s2.at[off], q2.at[off], to * MEMBERS + m
        )

    def round2_in(off):
        frm = (g + groups - off) % groups
        part = pl.ds(pl.multiple_of(jnp.where(g > frm, 0, SLICE), SLICE), 2 * SLICE)
        return remote(
            msg2.at[part], r2.at[frm, part], s2.at[off], q2.at[off], frm * MEMBERS + m
        )

    for off in range(1, groups):
        round2(off).start()
    for b in range(half, blocks):
        intra(b)
    cin[...] = jnp.zeros((SLICE, INNER), F32)
    ain[...] = jnp.zeros((SLICE, INNER), F32)
    for off in range(1, groups):
        round2_in(off).wait_recv()
    for q in range(groups):
        @pl.when(q < g)
        def _(q=q):
            d = unpack_decay(r2[q, pl.ds(SLICE, SLICE)])
            cin[...] = d * cin[...] + r2[q, pl.ds(0, SLICE)].astype(F32)
    for q in reversed(range(groups)):
        @pl.when(q > g)
        def _(q=q):
            d = unpack_decay(r2[q, pl.ds(SLICE, SLICE)])
            ain[...] = d * ain[...] + r2[q, pl.ds(2 * SLICE, SLICE)].astype(F32)
    gs = cin[...]
    for i in range(MEMBERS):
        msg3[i, pl.ds(0, SLICE)] = gs.astype(BF16)
        gs = decays[i] * gs + r1[i, pl.ds(0, SLICE)].astype(F32)
    ga = ain[...]
    for i in reversed(range(MEMBERS)):
        msg3[i, pl.ds(SLICE, SLICE)] = ga.astype(BF16)
        ga = decays[i] * ga + r1[i, pl.ds(2 * SLICE, SLICE)].astype(F32)

    def round3(off):
        to = (m + off) % MEMBERS
        return remote(msg3.at[to], r3.at[m], s3.at[off], q3.at[off], base + to)

    def round3_in(off):
        frm = (m + MEMBERS - off) % MEMBERS
        return remote(msg3.at[frm], r3.at[frm], s3.at[off], q3.at[off], base + frm)

    for off in range(1, MEMBERS):
        round3(off).start()
    r3[m] = msg3[m]
    skip = mm(jnp.broadcast_to(skip_ref[...], (8, HEADS)), spread_f, 1, 0, EXACT)[:1]
    skip_sum = jnp.zeros((1, INNER), F32)
    for b in range(blocks):
        rows_b = pl.ds(b * BLOCK, BLOCK)
        skip_sum = skip_sum + jnp.sum(
            cot_ref[rows_b].astype(F32) * act[rows_b, pl.ds(0, INNER)].astype(F32),
            axis=0, keepdims=True,
        )
    prm[...] = jnp.zeros((8, CONV), F32)
    prm[pl.ds(7, 1), pl.ds(0, HEADS)] = mm(
        jnp.broadcast_to(skip_sum, (8, INNER)), spread_f, 1, 1, EXACT
    )[:1]
    for off in range(1, MEMBERS):
        round3_in(off).wait_recv()

    state = jnp.concatenate([r3[i, pl.ds(0, SLICE)].astype(F32) for i in range(MEMBERS)], axis=0)
    adj = jnp.concatenate([r3[i, pl.ds(SLICE, SLICE)].astype(F32) for i in range(MEMBERS)], axis=0)
    for b in range(blocks):
        part = pl.ds(b * STATE, STATE)
        fresh = fall_ref[pl.ds(b * 8, 1)] * (state + piece[part])
        piece[part] = state
        state = fresh
    tails = [None] * blocks
    for b in reversed(range(blocks)):
        part = pl.ds(b * STATE, STATE)
        after = state if b == blocks - 1 else piece[pl.ds((b + 1) * STATE, STATE)]
        tails[b] = jnp.sum(adj * after, axis=0, keepdims=True)
        lent = fall_ref[pl.ds(b * 8, 1)] * adj
        adj = lent + back[part]
        back[part] = lent

    def dz_copy():
        return remote(
            dz.at[pl.ds(0, 8)], dz_edge, dz_sem.at[0], dz_sem.at[1], jnp.maximum(me - 1, 0)
        )

    alog_sum = jnp.zeros((HEADS, BLOCK), F32)
    dtb_sum = jnp.zeros((HEADS, BLOCK), F32)
    last_row = iota((BLOCK, 1), 0) == BLOCK - 1
    for b in range(blocks):
        t0 = b * BLOCK
        here = pl.ds(t0, BLOCK)
        part = pl.ds(b * STATE, STATE)
        xtb, gtb = xt[here], gt[here]
        bc = act[here, pl.ds(INNER, 2 * STATE)]
        bm, cm = bc[:, :STATE], bc[:, STATE:]
        carry_b = piece[part].astype(BF16)
        lent_b = back[part].astype(BF16)
        u = u_ref[here] + mm(cm, carry_b, 1, 0)
        v = v_ref[here] + mm(bm, lent_b, 1, 0)
        taken = xtb.astype(F32) * v
        moved = gtb.astype(F32) * u - taken + jnp.where(last_row, tails[b], 0.0)
        gcum = per_head(moved)
        step_b = step_ref[:, here]
        grate = mm(gcum, tri, 1, 1, EXACT)
        gstep = per_head(taken) / step_b + neg_a * grate
        alog_sum = alog_sum + grate * (neg_a * step_b)
        graw = gstep * sig_ref[:, here]
        gdt_ref[:, here] = graw
        dtb_sum = dtb_sum + graw
        gact = fx[here] * v + skip * cot_ref[here].astype(F32)
        dz[here, pl.ds(0, INNER)] = gact * dsil[here, pl.ds(0, INNER)]
        ds = ds_ref[here]
        gb = mm(ds, cm, 0, 0) + mm(xtb, lent_b, 1, 1)
        gc = mm(ds, bm, 1, 0) + mm(gtb, carry_b, 1, 1)
        dz[here, pl.ds(INNER, 2 * STATE)] = (
            jnp.concatenate([gb, gc], axis=1) * dsil[here, pl.ds(INNER, 2 * STATE)]
        )
        if b == 0:
            @pl.when(me > 0)
            def _():
                dz_copy().start()

    ones = jnp.ones((8, BLOCK), F32)
    prm[pl.ds(5, 1), pl.ds(0, HEADS)] = mm(ones, dtb_sum, 1, 1, EXACT)[:1]
    prm[pl.ds(6, 1), pl.ds(0, HEADS)] = mm(ones, alog_sum, 1, 1, EXACT)[:1]
    for j in range(CONV // 128):
        lanes = pl.ds(j * 128, 128)
        total = [jnp.zeros((8, 128), F32) for _ in range(5)]
        for b in range(blocks):
            t0 = b * BLOCK
            grad = dz[pl.ds(t0, BLOCK), lanes]
            for k in range(4):
                total[k] = total[k] + jnp.sum(
                    (grad * xs[pl.ds(t0 + 5 + k, BLOCK), lanes]).reshape(BLOCK // 8, 8, 128), axis=0
                )
            total[4] = total[4] + jnp.sum(grad.reshape(BLOCK // 8, 8, 128), axis=0)
        for k in range(5):
            prm[pl.ds(k, 1), lanes] = jnp.sum(total[k], axis=0, keepdims=True)

    def sum1(off):
        to = (m + off) % MEMBERS
        return remote(prm, p1.at[m], s4.at[off], q4.at[off], base + to)

    def sum1_in(off):
        frm = (m + MEMBERS - off) % MEMBERS
        return remote(prm, p1.at[frm], s4.at[off], q4.at[off], base + frm)

    def sum2(off):
        to = (g + off) % groups
        return remote(p2s, p2.at[g], s5.at[off], q5.at[off], to * MEMBERS + m)

    def sum2_in(off):
        frm = (g + groups - off) % groups
        return remote(p2s, p2.at[frm], s5.at[off], q5.at[off], frm * MEMBERS + m)

    for off in range(1, MEMBERS):
        sum1(off).start()
    p1[m] = prm[...]

    def data_grad(b):
        t0 = b * BLOCK
        for j in range(CONV // 128):
            lanes = pl.ds(j * 128, 128)
            total = w_ref[pl.ds(0, 1), lanes] * dz[pl.ds(t0 + 3, BLOCK), lanes]
            for k in range(1, 4):
                total = total + w_ref[pl.ds(k, 1), lanes] * dz[pl.ds(t0 + 3 - k, BLOCK), lanes]
            gx_ref[pl.ds(t0, BLOCK), lanes] = total.astype(BF16)

    for b in range(half):
        data_grad(b)
    for off in range(1, MEMBERS):
        sum1_in(off).wait_recv()
    p2s[...] = (p1[0] + p1[1]) + (p1[2] + p1[3])
    for off in range(1, groups):
        sum2(off).start()
    p2[g] = p2s[...]
    dz[pl.ds(rows, 8)] = jnp.zeros((8, CONV), F32)

    @pl.when(me < n - 1)
    def _():
        dz_copy().wait_recv()
        dz[pl.ds(rows, 8)] = dz_edge[...]

    for b in range(half, blocks):
        data_grad(b)
    for off in range(1, groups):
        sum2_in(off).wait_recv()
    total = p2[0]
    for q in range(1, groups):
        total = total + p2[q]
    gw_ref[...] = total[:4]
    gbias_ref[...] = total[4:5]
    gdtb_ref[...] = total[5:6, :HEADS]
    galog_ref[...] = total[6:7, :HEADS]
    gskip_ref[...] = total[7:8, :HEADS]

    @pl.when(me < n - 1)
    def _():
        edge_copy().wait_send()

    @pl.when(me > 0)
    def _():
        dz_copy().wait_send()

    for off in range(1, MEMBERS):
        round1(off).wait_send()
        round3(off).wait_send()
        sum1(off).wait_send()
    for off in range(1, groups):
        round2(off).wait_send()
        sum2(off).wait_send()


def local(n, xbc, dt_raw, cotangent, conv_weight, conv_bias, dt_bias, a_log, d_skip):
    rows = xbc.shape[0]
    blocks = rows // BLOCK
    groups = n // MEMBERS
    vmem = pl.BlockSpec(memory_space=pltpu.VMEM)
    dma = pltpu.SemaphoreType.DMA
    outs = pl.pallas_call(
        functools.partial(kernel, n),
        out_shape=(
            jax.ShapeDtypeStruct((rows, CONV), BF16),
            jax.ShapeDtypeStruct((HEADS, rows), F32),
            jax.ShapeDtypeStruct((4, CONV), F32),
            jax.ShapeDtypeStruct((1, CONV), F32),
            jax.ShapeDtypeStruct((1, HEADS), F32),
            jax.ShapeDtypeStruct((1, HEADS), F32),
            jax.ShapeDtypeStruct((1, HEADS), F32),
        ),
        in_specs=[vmem] * 8,
        out_specs=(vmem,) * 7,
        scratch_shapes=[
            pltpu.VMEM((rows + 8, CONV), F32),
            pltpu.VMEM((16, CONV), BF16),
            pltpu.VMEM((rows, CONV), BF16),
            pltpu.VMEM((rows, CONV), F32),
            pltpu.VMEM((rows, INNER), BF16),
            pltpu.VMEM((rows, INNER), BF16),
            pltpu.VMEM((rows, INNER), F32),
            pltpu.VMEM((rows, INNER), F32),
            pltpu.VMEM((rows, INNER), F32),
            pltpu.VMEM((rows, BLOCK), BF16),
            pltpu.VMEM((blocks * STATE, INNER), F32),
            pltpu.VMEM((blocks * STATE, INNER), F32),
            pltpu.VMEM((blocks * 8, INNER), F32),
            pltpu.VMEM((HEADS, rows), F32),
            pltpu.VMEM((HEADS, rows), F32),
            pltpu.VMEM((MEMBERS, 3 * SLICE, INNER), BF16),
            pltpu.VMEM((MEMBERS, 3 * SLICE, INNER), BF16),
            pltpu.VMEM((3 * SLICE, INNER), BF16),
            pltpu.VMEM((groups, 3 * SLICE, INNER), BF16),
            pltpu.VMEM((MEMBERS, 2 * SLICE, INNER), BF16),
            pltpu.VMEM((MEMBERS, 2 * SLICE, INNER), BF16),
            pltpu.VMEM((SLICE, INNER), F32),
            pltpu.VMEM((SLICE, INNER), F32),
            pltpu.VMEM((rows + 8, CONV), F32),
            pltpu.VMEM((8, CONV), F32),
            pltpu.VMEM((8, CONV), F32),
            pltpu.VMEM((MEMBERS, 8, CONV), F32),
            pltpu.VMEM((8, CONV), F32),
            pltpu.VMEM((groups, 8, CONV), F32),
            dma((2,)),
            dma((MEMBERS,)), dma((MEMBERS,)),
            dma((groups,)), dma((groups,)),
            dma((MEMBERS,)), dma((MEMBERS,)),
            dma((2,)),
            dma((MEMBERS,)), dma((MEMBERS,)),
            dma((groups,)), dma((groups,)),
        ],
        compiler_params=pltpu.CompilerParams(
            collective_id=0, has_side_effects=True, vmem_limit_bytes=56 * 1024 * 1024
        ),
        cost_estimate=pl.CostEstimate(
            flops=2 * 10**9, bytes_accessed=5 * 10**6, transcendentals=10**6
        ),
        name="mixer",
    )(
        xbc, dt_raw, cotangent, conv_weight, conv_bias.reshape(1, CONV),
        dt_bias.reshape(1, HEADS), a_log.reshape(1, HEADS), d_skip.reshape(1, HEADS),
    )
    return (
        outs[0], outs[1], outs[2], outs[3].reshape(CONV), outs[4].reshape(HEADS),
        outs[5].reshape(HEADS), outs[6].reshape(HEADS),
    )


def solution(mesh):
    sequence = P(("groups", "seq"), None)
    return jax.shard_map(
        functools.partial(local, mesh.shape["seq"]),
        mesh=mesh,
        in_specs=(sequence, P(None, ("groups", "seq")), sequence, P(), P(), P(), P(), P()),
        out_specs=(
            sequence, P(None, ("groups", "seq")), P("groups", None),
            P("groups"), P("groups"), P("groups"), P("groups"),
        ),
        check_vma=False,
    )
```

time: 595 us -> 58.8 us (0.10); the launches traced: 588 us -> 58.5 us
  local copies, waits for them, and re-layouts: 158 us -> 6.69 us
  other arithmetic: 130 us -> 1.31 us
  waiting for transfers between devices: 96.7 us -> 0 us
  blocking collectives: 94.5 us -> 0 us
  matrix products: 87.2 us -> 0 us
  Pallas kernels: 0 us -> 49.9 us
  between operations: 15.2 us -> 0.65 us
    all_gather x2 -> x0, waiting for transfers between devices: 96.7 us -> none  [the longest x1 77.7 us: carried_in(): lax.all_gather(part.astype(kind), axis)]
    dot_general x56 -> x0, matrix products: 87.2 us -> none  [the longest x24 40.3 us: block_state(): jnp.einsum('tn,thp->hnp', b_part.astype(jnp.float32), scaled, precision=l...]
    psum x1 -> x0, blocking collectives: 60.7 us -> none  [local(): lax.psum((grad_weight, grad_bias, grad_dtbias, grad_alog, grad_skip), 'seq')]
    dynamic_slice x56 -> x0, local copies, waits for them, and re-layouts: 50.6 us -> none  [the longest x24 29.4 us: outputs(): lax.scan(outputs_advance, state_in, to_blocks(x_part, b_part, c_part, ste...]
    pallas_call x0 -> x1, Pallas kernels: none -> 49.9 us  [local(): pl.pallas_call(functools.partial(kernel, n), out_shape=(jax.ShapeDtypeStr...]
    unnamed x1 -> x0, blocking collectives: 33.7 us -> none
    dynamic_update_slice x36 -> x0, other arithmetic: 32.7 us -> none  [the longest x32 28.8 us: local_state(): lax.scan(local_advance, start, (blocked[0], blocked[1], blocked[3], block...]
    reduce_sum x31 -> x0, other arithmetic: 29.8 us -> none  [the longest x4 7.94 us: outputs_advance(): return (decay[:, None, None] * carried + state_piece, result)]
  transfers between devices with their start and end apart: 4 -> 0, of which waited for: 2 -> 0; matrix products, arithmetic and copies ran while one was open for 6% -> 0% of each run, Pallas kernels for 0% -> 0%
where the time goes in v1:
time: 58.8 us; the launch traced here: 58.5 us
  Pallas kernels  49.9 us (85%)
  local copies, waits for them, and re-layouts  6.69 us (11%)
  other arithmetic  1.31 us (2%)
  between operations  0.65 us (1%)
    pallas_call x1, Pallas kernels, local(): pl.pallas_call(functools.partial(kernel, n), out_shape=(jax.ShapeDtypeStr...  49.9 us
    unnamed x16, local copies, waits for them, and re-layouts  5.4 us
    pallas_call x1, other arithmetic, local(): pl.pallas_call(functools.partial(kernel, n), out_shape=(jax.ShapeDtypeStr...  1.31 us
    reshape x1, local copies, waits for them, and re-layouts, local(): conv_bias.reshape(1, CONV)  1.29 us

profile of v1, /device:TPU:0, one launch (start us, length us, event | category | flops | bytes accessed | tf_op | source)
XLA Modules:
  0.0 58.5 jit_solution(5017781050855900757)
XLA Ops:
  0.6 1.3 %reshape.38.bias_ref = f32[1,1408]{1,0:T(1,128)} reshape(f32[1408]{0:T(1024)} %param.12) | data formatting | bytes 11264 | tf_op jit(solution)/shard_map/reshape | solution.py:495
  1.9 49.9 %mixer.1 = (bf16[512,1408]{1,0:T(8,128)(2,1)}, f32[40,512]{1,0:T(8,128)}, f32[4,1408]{1,0:T(4,128)}, f32[1,1408]{1,0:T(1,128)}, f32[1,40]{1,0:T(1,128)}, /*index=5*/f32[1,40]{1,0:T(1,128)}, f32[1,40]{1,0:T(1,128)}) custom-call(bf16[512,1408]{1,0:T(8,128)(2,1)} %x_ref.1, f32[40,512]{1,0:T(8,128)} %dt_ref.1, bf16[512,1280]{1,0:T(8,128)(2,1)} %cot_ref.1, ...), custom_call_target="tpu_custom_call" | custom-call | flops 2000000000 | bytes 5000000 | tf_op jit(solution)/shard_map/mixer/pallas_call | solution.py:436
  51.8 1.3 %reduce = f32[1408]{0:T(1024)} reduce(f32[1,1408]{1,0:T(1,128)} %get-tuple-element.17, f32[]{:T(128)} %constant), dimensions={0}, to_apply=%get-tuple-element.17.reduce_sub_computation | reduce | bytes 11268 | tf_op jit(solution)/shard_map/mixer/pallas_call | solution.py:436
  53.1 0.0 copy-start
  53.1 0.0 copy-start.1
  53.1 0.0 copy-start.4
  53.1 0.0 copy-start.3
  53.1 0.0 copy-start.2
  53.1 2.6 %copy.21 = bf16[512,1408]{1,0:T(8,128)(2,1)} copy(bf16[512,1408]{1,0:T(8,128)(2,1)} %get-tuple-element.28) | data formatting | bytes 2883584
  55.7 0.0 copy-done
  55.7 0.6 %copy.22 = f32[40,512]{1,0:T(8,128)} copy(f32[40,512]{1,0:T(8,128)S(1)} %copy-done) | data formatting | bytes 163840
  56.4 0.0 copy-done.1
  56.4 0.6 %copy.23 = f32[4,1408]{1,0:T(4,128)} copy(f32[4,1408]{1,0:T(4,128)S(1)} %copy-done.1) | data formatting | bytes 45056
  57.0 0.0 copy-done.4
  57.0 0.5 copy.24
  57.5 0.0 copy-done.3
  57.5 0.5 copy.25
  58.0 0.0 copy-done.2
  58.0 0.5 copy.26
Async XLA Ops:
  53.1 2.6 %copy-start = (f32[40,512]{1,0:T(8,128)S(1)}, f32[40,512]{1,0:T(8,128)}, u32[]{:S(2)}) copy-start(f32[40,512]{1,0:T(8,128)} %get-tuple-element.29) | copy-start | bytes 245764
  53.1 3.3 %copy-start.1 = (f32[4,1408]{1,0:T(4,128)S(1)}, f32[4,1408]{1,0:T(4,128)}, u32[]{:S(2)}) copy-start(f32[4,1408]{1,0:T(4,128)} %get-tuple-element.30) | copy-start | bytes 67588
  53.1 3.9 %copy-start.4 = (f32[1,40]{1,0:T(1,128)S(1)}, f32[1,40]{1,0:T(1,128)}, u32[]{:S(2)}) copy-start(f32[1,40]{1,0:T(1,128)} %get-tuple-element.18) | copy-start | bytes 484
  53.1 4.4 %copy-start.3 = (f32[1,40]{1,0:T(1,128)S(1)}, f32[1,40]{1,0:T(1,128)}, u32[]{:S(2)}) copy-start(f32[1,40]{1,0:T(1,128)} %get-tuple-element.19) | copy-start | bytes 484
  53.1 4.9 %copy-start.2 = (f32[1,40]{1,0:T(1,128)S(1)}, f32[1,40]{1,0:T(1,128)}, u32[]{:S(2)}) copy-start(f32[1,40]{1,0:T(1,128)} %get-tuple-element.20) | copy-start | bytes 484

commit v2 on v1

--- a/solution.py
+++ b/solution.py
@@ -15,6 +15,8 @@
 CONV = INNER + 2 * STATE
 MEMBERS = 4
 SLICE = STATE // MEMBERS
+CUTS = 2
+WIDTH = INNER // CUTS
 F32 = jnp.float32
 BF16 = jnp.bfloat16
 EXACT = lax.Precision.HIGHEST
@@ -44,10 +46,11 @@
 def kernel(
     n,
     x_ref, dt_ref, cot_ref, w_ref, bias_ref, dtb_ref, alog_ref, skip_ref,
-    gx_ref, gdt_ref, gw_ref, gbias_ref, gdtb_ref, galog_ref, gskip_ref,
+    gx_ref, gdt_ref, sums_ref,
     xs, edge, act, dsil, xt, gt, fx, u_ref, v_ref, ds_ref, piece, back, fall_ref,
     step_ref, sig_ref, msg, r1, msg2, r2, msg3, r3, cin, ain, dz, dz_edge, prm, p1, p2s, p2,
-    edge_sem, s1, q1, s2, q2, s3, q3, dz_sem, s4, q4, s5, q5,
+    dec, dall, dexp,
+    edge_sem, s1, q1, s2, q2, s3, q3, dz_sem, s4, q4, s5, q5, s6, q6,
 ):
     rows = x_ref.shape[0]
     blocks = rows // BLOCK
@@ -108,6 +111,32 @@
         high, low = split(v)
         return mm(spread1, high, 1, 1) + mm(spread1, low, 1, 1)
 
+    total_rate = mm(jnp.ones((8, rows), F32), neg_a * step, 1, 1, EXACT)
+    dec[...] = jnp.zeros((8, 128), F32)
+    dec[:, pl.ds(0, HEADS)] = jnp.exp(total_rate)
+
+    def decay_out(off):
+        return remote(dec, dall.at[me], s6.at[off], q6.at[off], (me + off) % n)
+
+    def decay_in(off):
+        frm = (me + n - off) % n
+        return remote(dec, dall.at[frm], s6.at[off], q6.at[off], frm)
+
+    def decay_start(off, carry):
+        decay_out(off).start()
+        return carry
+
+    def decay_wait(off, carry):
+        decay_in(off).wait_recv()
+        return carry
+
+    def decay_sent(off, carry):
+        decay_out(off).wait_send()
+        return carry
+
+    lax.fori_loop(1, n, decay_start, 0)
+    dall[me] = dec[...]
+
     xs[pl.ds(8, rows)] = x_ref[...].astype(F32)
     for b in list(range(1, blocks)) + [0]:
         t0 = b * BLOCK
@@ -121,7 +150,7 @@
 
         for j in range(CONV // 128):
             lanes = pl.ds(j * 128, 128)
-            z = jnp.broadcast_to(bias_ref[:, lanes], (BLOCK, 128))
+            z = jnp.broadcast_to(bias_ref[lanes].reshape(1, 128), (BLOCK, 128))
             for k in range(4):
                 z = z + w_ref[pl.ds(k, 1), lanes] * xs[pl.ds(t0 + 5 + k, BLOCK), lanes]
             s = 1.0 / (1.0 + jnp.exp(-z))
@@ -144,42 +173,28 @@
 
     state = jnp.zeros((STATE, INNER), F32)
     adj = jnp.zeros((STATE, INNER), F32)
-    decay = jnp.ones((1, INNER), F32)
     for b in range(blocks):
-        fall = fall_ref[pl.ds(b * 8, 1)]
-        state = fall * (state + piece[pl.ds(b * STATE, STATE)])
-        decay = decay * fall
+        state = fall_ref[pl.ds(b * 8, 1)] * (state + piece[pl.ds(b * STATE, STATE)])
     for b in reversed(range(blocks)):
         adj = fall_ref[pl.ds(b * 8, 1)] * adj + back[pl.ds(b * STATE, STATE)]
-
-    def pack_decay(d):
-        d16 = jnp.broadcast_to(d, (SLICE, INNER))
-        high = d16.astype(BF16).astype(F32)
-        rest = d16 - high
-        mid = rest.astype(BF16).astype(F32)
-        low = rest - mid
-        at = iota((SLICE, INNER), 0)
-        return jnp.where(at == 0, high, jnp.where(at == 1, mid, jnp.where(at == 2, low, 0.0))).astype(BF16)
-
-    def unpack_decay(d):
-        return jnp.sum(d.astype(F32), axis=0, keepdims=True)
-
-    packed = pack_decay(decay)
+    top, low = pl.ds(0, SLICE), pl.ds(SLICE, SLICE)
     for j in range(MEMBERS):
-        msg[j, pl.ds(0, SLICE)] = state[j * SLICE : (j + 1) * SLICE].astype(BF16)
-        msg[j, pl.ds(SLICE, SLICE)] = packed
-        msg[j, pl.ds(2 * SLICE, SLICE)] = adj[j * SLICE : (j + 1) * SLICE].astype(BF16)
-
-    def round1(off):
+        for c in range(CUTS):
+            part = slice(c * WIDTH, (c + 1) * WIDTH)
+            msg[j, c, top] = state[j * SLICE : (j + 1) * SLICE, part].astype(BF16)
+            msg[j, c, low] = adj[j * SLICE : (j + 1) * SLICE, part].astype(BF16)
+
+    def round1(off, c):
         to = (m + off) % MEMBERS
-        return remote(msg.at[to], r1.at[m], s1.at[off], q1.at[off], base + to)
-
-    def round1_in(off):
+        return remote(msg.at[to, c], r1.at[m, c], s1.at[off, c], q1.at[off, c], base + to)
+
+    def round1_in(off, c):
         frm = (m + MEMBERS - off) % MEMBERS
-        return remote(msg.at[frm], r1.at[frm], s1.at[off], q1.at[off], base + frm)
-
-    for off in range(1, MEMBERS):
-        round1(off).start()
+        return remote(msg.at[frm, c], r1.at[frm, c], s1.at[off, c], q1.at[off, c], base + frm)
+
+    for c in range(CUTS):
+        for off in range(1, MEMBERS):
+            round1(off, c).start()
     r1[m] = msg[m]
 
     def intra(b):
@@ -196,73 +211,86 @@
     for b in range(half):
         intra(b)
 
-    for off in range(1, MEMBERS):
-        round1_in(off).wait_recv()
-    decays = [unpack_decay(r1[i, pl.ds(SLICE, SLICE)]) for i in range(MEMBERS)]
-    gs = jnp.zeros((SLICE, INNER), F32)
-    ga = jnp.zeros((SLICE, INNER), F32)
-    gd = jnp.ones((1, INNER), F32)
-    for i in range(MEMBERS):
-        gs = decays[i] * gs + r1[i, pl.ds(0, SLICE)].astype(F32)
-        gd = gd * decays[i]
-    for i in reversed(range(MEMBERS)):
-        ga = decays[i] * ga + r1[i, pl.ds(2 * SLICE, SLICE)].astype(F32)
-    msg2[pl.ds(0, SLICE)] = gs.astype(BF16)
-    msg2[pl.ds(SLICE, SLICE)] = pack_decay(gd)
-    msg2[pl.ds(2 * SLICE, SLICE)] = ga.astype(BF16)
-
-    def round2(off):
+    lax.fori_loop(1, n, decay_wait, 0)
+    lines = [dall[base + i] for i in range(MEMBERS)]
+    for q in range(groups):
+        own = dall[q * MEMBERS]
+        for i in range(1, MEMBERS):
+            own = own * dall[q * MEMBERS + i]
+        lines.append(own)
+    spread128 = jnp.where((iota((128, INNER), 1) >> 5) == iota((128, INNER), 0), 1.0, 0.0)
+    dexp[...] = mm(jnp.concatenate(lines, axis=0), spread128, 1, 0, EXACT)
+
+    def round2(off, c):
         to = (g + off) % groups
-        part = pl.ds(pl.multiple_of(jnp.where(to > g, 0, SLICE), SLICE), 2 * SLICE)
+        part = pl.ds(pl.multiple_of(jnp.where(to > g, 0, SLICE), SLICE), SLICE)
         return remote(
-            msg2.at[part], r2.at[g, part], s2.at[off], q2.at[off], to * MEMBERS + m
-        )
-
-    def round2_in(off):
+            msg2.at[c, part], r2.at[g, c, part], s2.at[off, c], q2.at[off, c], to * MEMBERS + m
+        )
+
+    def round2_in(off, c):
         frm = (g + groups - off) % groups
-        part = pl.ds(pl.multiple_of(jnp.where(g > frm, 0, SLICE), SLICE), 2 * SLICE)
+        part = pl.ds(pl.multiple_of(jnp.where(g > frm, 0, SLICE), SLICE), SLICE)
         return remote(
-            msg2.at[part], r2.at[frm, part], s2.at[off], q2.at[off], frm * MEMBERS + m
-        )
-
-    for off in range(1, groups):
-        round2(off).start()
-    for b in range(half, blocks):
+            msg2.at[c, part], r2.at[frm, c, part], s2.at[off, c], q2.at[off, c],
+            frm * MEMBERS + m,
+        )
+
+    for c in range(CUTS):
+        lanes = pl.ds(c * WIDTH, WIDTH)
+        for off in range(1, MEMBERS):
+            round1_in(off, c).wait_recv()
+        gs = r1[0, c, top].astype(F32)
+        for i in range(1, MEMBERS):
+            gs = dexp[pl.ds(i * 8, 1), lanes] * gs + r1[i, c, top].astype(F32)
+        ga = r1[MEMBERS - 1, c, low].astype(F32)
+        for i in reversed(range(MEMBERS - 1)):
+            ga = dexp[pl.ds(i * 8, 1), lanes] * ga + r1[i, c, low].astype(F32)
+        msg2[c, top] = gs.astype(BF16)
+        msg2[c, low] = ga.astype(BF16)
+        for off in range(1, groups):
+            round2(off, c).start()
+
+    for b in range(half, blocks - 1):
         intra(b)
+
+    def round3(off, c):
+        to = (m + off) % MEMBERS
+        return remote(msg3.at[to, c], r3.at[m, c], s3.at[off, c], q3.at[off, c], base + to)
+
+    def round3_in(off, c):
+        frm = (m + MEMBERS - off) % MEMBERS
+        return remote(msg3.at[frm, c], r3.at[frm, c], s3.at[off, c], q3.at[off, c], base + frm)
+
     cin[...] = jnp.zeros((SLICE, INNER), F32)
     ain[...] = jnp.zeros((SLICE, INNER), F32)
-    for off in range(1, groups):
-        round2_in(off).wait_recv()
-    for q in range(groups):
-        @pl.when(q < g)
-        def _(q=q):
-            d = unpack_decay(r2[q, pl.ds(SLICE, SLICE)])
-            cin[...] = d * cin[...] + r2[q, pl.ds(0, SLICE)].astype(F32)
-    for q in reversed(range(groups)):
-        @pl.when(q > g)
-        def _(q=q):
-            d = unpack_decay(r2[q, pl.ds(SLICE, SLICE)])
-            ain[...] = d * ain[...] + r2[q, pl.ds(2 * SLICE, SLICE)].astype(F32)
-    gs = cin[...]
-    for i in range(MEMBERS):
-        msg3[i, pl.ds(0, SLICE)] = gs.astype(BF16)
-        gs = decays[i] * gs + r1[i, pl.ds(0, SLICE)].astype(F32)
-    ga = ain[...]
-    for i in reversed(range(MEMBERS)):
-        msg3[i, pl.ds(SLICE, SLICE)] = ga.astype(BF16)
-        ga = decays[i] * ga + r1[i, pl.ds(2 * SLICE, SLICE)].astype(F32)
-
-    def round3(off):
-        to = (m + off) % MEMBERS
-        return remote(msg3.at[to], r3.at[m], s3.at[off], q3.at[off], base + to)
-
-    def round3_in(off):
-        frm = (m + MEMBERS - off) % MEMBERS
-        return remote(msg3.at[frm], r3.at[frm], s3.at[off], q3.at[off], base + frm)
-
-    for off in range(1, MEMBERS):
-        round3(off).start()
+    for c in range(CUTS):
+        lanes = pl.ds(c * WIDTH, WIDTH)
+        for off in range(1, groups):
+            round2_in(off, c).wait_recv()
+        for q in range(groups):
+            @pl.when(q < g)
+            def _(q=q):
+                d = dexp[pl.ds((MEMBERS + q) * 8, 1), lanes]
+                cin[:, lanes] = d * cin[:, lanes] + r2[q, c, top].astype(F32)
+        for q in reversed(range(groups)):
+            @pl.when(q > g)
+            def _(q=q):
+                d = dexp[pl.ds((MEMBERS + q) * 8, 1), lanes]
+                ain[:, lanes] = d * ain[:, lanes] + r2[q, c, low].astype(F32)
+        gs = cin[:, lanes]
+        for i in range(MEMBERS):
+            msg3[i, c, top] = gs.astype(BF16)
+            gs = dexp[pl.ds(i * 8, 1), lanes] * gs + r1[i, c, top].astype(F32)
+        ga = ain[:, lanes]
+        for i in reversed(range(MEMBERS)):
+            msg3[i, c, low] = ga.astype(BF16)
+            ga = dexp[pl.ds(i * 8, 1), lanes] * ga + r1[i, c, low].astype(F32)
+        for off in range(1, MEMBERS):
+            round3(off, c).start()
     r3[m] = msg3[m]
+    for b in range(blocks - 1, blocks):
+        intra(b)
     skip = mm(jnp.broadcast_to(skip_ref[...], (8, HEADS)), spread_f, 1, 0, EXACT)[:1]
     skip_sum = jnp.zeros((1, INNER), F32)
     for b in range(blocks):
@@ -275,11 +303,21 @@
     prm[pl.ds(7, 1), pl.ds(0, HEADS)] = mm(
         jnp.broadcast_to(skip_sum, (8, INNER)), spread_f, 1, 1, EXACT
     )[:1]
-    for off in range(1, MEMBERS):
-        round3_in(off).wait_recv()
-
-    state = jnp.concatenate([r3[i, pl.ds(0, SLICE)].astype(F32) for i in range(MEMBERS)], axis=0)
-    adj = jnp.concatenate([r3[i, pl.ds(SLICE, SLICE)].astype(F32) for i in range(MEMBERS)], axis=0)
+    for c in range(CUTS):
+        for off in range(1, MEMBERS):
+            round3_in(off, c).wait_recv()
+
+    def gathered(half_of):
+        return jnp.concatenate(
+            [
+                jnp.concatenate([r3[i, c, half_of].astype(F32) for c in range(CUTS)], axis=1)
+                for i in range(MEMBERS)
+            ],
+            axis=0,
+        )
+
+    state = gathered(top)
+    adj = gathered(low)
     for b in range(blocks):
         part = pl.ds(b * STATE, STATE)
         fresh = fall_ref[pl.ds(b * 8, 1)] * (state + piece[part])
@@ -404,11 +442,7 @@
     total = p2[0]
     for q in range(1, groups):
         total = total + p2[q]
-    gw_ref[...] = total[:4]
-    gbias_ref[...] = total[4:5]
-    gdtb_ref[...] = total[5:6, :HEADS]
-    galog_ref[...] = total[6:7, :HEADS]
-    gskip_ref[...] = total[7:8, :HEADS]
+    sums_ref[...] = total
 
     @pl.when(me < n - 1)
     def _():
@@ -419,12 +453,25 @@
         dz_copy().wait_send()
 
     for off in range(1, MEMBERS):
-        round1(off).wait_send()
-        round3(off).wait_send()
+        for c in range(CUTS):
+            round1(off, c).wait_send()
+            round3(off, c).wait_send()
         sum1(off).wait_send()
     for off in range(1, groups):
-        round2(off).wait_send()
+        for c in range(CUTS):
+            round2(off, c).wait_send()
         sum2(off).wait_send()
+    lax.fori_loop(1, n, decay_sent, 0)
+
+
+def finish(gx_in, gdt_in, sums, gx_ref, gdt_ref, gw_ref, gbias_ref, gdtb_ref, galog_ref, gskip_ref):
+    gx_ref[...] = gx_in[...]
+    gdt_ref[...] = gdt_in[...]
+    gw_ref[...] = sums[pl.ds(0, 4)]
+    gbias_ref[...] = sums[pl.ds(4, 1)].reshape(CONV)
+    gdtb_ref[...] = sums[pl.ds(5, 1), pl.ds(0, HEADS)].reshape(HEADS)
+    galog_ref[...] = sums[pl.ds(6, 1), pl.ds(0, HEADS)].reshape(HEADS)
+    gskip_ref[...] = sums[pl.ds(7, 1), pl.ds(0, HEADS)].reshape(HEADS)
 
 
 def local(n, xbc, dt_raw, cotangent, conv_weight, conv_bias, dt_bias, a_log, d_skip):
@@ -438,14 +485,10 @@
         out_shape=(
             jax.ShapeDtypeStruct((rows, CONV), BF16),
             jax.ShapeDtypeStruct((HEADS, rows), F32),
-            jax.ShapeDtypeStruct((4, CONV), F32),
-            jax.ShapeDtypeStruct((1, CONV), F32),
-            jax.ShapeDtypeStruct((1, HEADS), F32),
-            jax.ShapeDtypeStruct((1, HEADS), F32),
-            jax.ShapeDtypeStruct((1, HEADS), F32),
+            jax.ShapeDtypeStruct((8, CONV), F32),
         ),
         in_specs=[vmem] * 8,
-        out_specs=(vmem,) * 7,
+        out_specs=(vmem,) * 3,
         scratch_shapes=[
             pltpu.VMEM((rows + 8, CONV), F32),
             pltpu.VMEM((16, CONV), BF16),
@@ -462,12 +505,12 @@
             pltpu.VMEM((blocks * 8, INNER), F32),
             pltpu.VMEM((HEADS, rows), F32),
             pltpu.VMEM((HEADS, rows), F32),
-            pltpu.VMEM((MEMBERS, 3 * SLICE, INNER), BF16),
-            pltpu.VMEM((MEMBERS, 3 * SLICE, INNER), BF16),
-            pltpu.VMEM((3 * SLICE, INNER), BF16),
-            pltpu.VMEM((groups, 3 * SLICE, INNER), BF16),
-            pltpu.VMEM((MEMBERS, 2 * SLICE, INNER), BF16),
-            pltpu.VMEM((MEMBERS, 2 * SLICE, INNER), BF16),
+            pltpu.VMEM((MEMBERS, CUTS, 2 * SLICE, WIDTH), BF16),
+            pltpu.VMEM((MEMBERS, CUTS, 2 * SLICE, WIDTH), BF16),
+            pltpu.VMEM((CUTS, 2 * SLICE, WIDTH), BF16),
+            pltpu.VMEM((groups, CUTS, 2 * SLICE, WIDTH), BF16),
+            pltpu.VMEM((MEMBERS, CUTS, 2 * SLICE, WIDTH), BF16),
+            pltpu.VMEM((MEMBERS, CUTS, 2 * SLICE, WIDTH), BF16),
             pltpu.VMEM((SLICE, INNER), F32),
             pltpu.VMEM((SLICE, INNER), F32),
             pltpu.VMEM((rows + 8, CONV), F32),
@@ -476,13 +519,17 @@
             pltpu.VMEM((MEMBERS, 8, CONV), F32),
             pltpu.VMEM((8, CONV), F32),
             pltpu.VMEM((groups, 8, CONV), F32),
+            pltpu.VMEM((8, 128), F32),
+            pltpu.VMEM((n, 8, 128), F32),
+            pltpu.VMEM(((MEMBERS + groups) * 8, INNER), F32),
+            dma((2,)),
+            dma((MEMBERS, CUTS)), dma((MEMBERS, CUTS)),
+            dma((groups, CUTS)), dma((groups, CUTS)),
+            dma((MEMBERS, CUTS)), dma((MEMBERS, CUTS)),
             dma((2,)),
             dma((MEMBERS,)), dma((MEMBERS,)),
             dma((groups,)), dma((groups,)),
-            dma((MEMBERS,)), dma((MEMBERS,)),
-            dma((2,)),
-            dma((MEMBERS,)), dma((MEMBERS,)),
-            dma((groups,)), dma((groups,)),
+            dma((n,)), dma((n,)),
         ],
         compiler_params=pltpu.CompilerParams(
             collective_id=0, has_side_effects=True, vmem_limit_bytes=56 * 1024 * 1024
@@ -492,13 +539,25 @@
         ),
         name="mixer",
     )(
-        xbc, dt_raw, cotangent, conv_weight, conv_bias.reshape(1, CONV),
+        xbc, dt_raw, cotangent, conv_weight, conv_bias,
         dt_bias.reshape(1, HEADS), a_log.reshape(1, HEADS), d_skip.reshape(1, HEADS),
     )
-    return (
-        outs[0], outs[1], outs[2], outs[3].reshape(CONV), outs[4].reshape(HEADS),
-        outs[5].reshape(HEADS), outs[6].reshape(HEADS),
-    )
+    return pl.pallas_call(
+        finish,
+        out_shape=(
+            jax.ShapeDtypeStruct((rows, CONV), BF16),
+            jax.ShapeDtypeStruct((HEADS, rows), F32),
+            jax.ShapeDtypeStruct((4, CONV), F32),
+            jax.ShapeDtypeStruct((CONV,), F32),
+            jax.ShapeDtypeStruct((HEADS,), F32),
+            jax.ShapeDtypeStruct((HEADS,), F32),
+            jax.ShapeDtypeStruct((HEADS,), F32),
+        ),
+        in_specs=[vmem] * 3,
+        out_specs=(vmem,) * 7,
+        compiler_params=pltpu.CompilerParams(vmem_limit_bytes=56 * 1024 * 1024),
+        name="finish",
+    )(*outs)
 
 
 def solution(mesh):

time: 58.8 us -> 49.2 us (0.84)
  local copies, waits for them, and re-layouts: 6.69 us -> 0 us
  Pallas kernels: 49.9 us -> 48.3 us
  other arithmetic: 1.31 us -> 0 us
    unnamed x16 -> x0, local copies, waits for them, and re-layouts: 5.4 us -> none
    pallas_call x1, Pallas kernels: 49.9 us -> 45.7 us  [local(): pl.pallas_call(functools.partial(kernel, n), out_shape=(jax.ShapeDtypeStr...]
    pallas_call x0 -> x1, Pallas kernels: none -> 2.63 us  [local(): pl.pallas_call(finish, out_shape=(jax.ShapeDtypeStruct((rows, CONV), BF16...]
    pallas_call x1 -> x0, other arithmetic: 1.31 us -> none  [local(): pl.pallas_call(functools.partial(kernel, n), out_shape=(jax.ShapeDtypeStr...]
    reshape x1 -> x0, local copies, waits for them, and re-layouts: 1.29 us -> none  [local(): conv_bias.reshape(1, CONV)]
where the time goes in v2:
time: 49.2 us; the launch traced here: 49 us
  Pallas kernels  48.3 us (98%)
  between operations  0.64 us (1%)
    pallas_call x1, Pallas kernels, local(): pl.pallas_call(functools.partial(kernel, n), out_shape=(jax.ShapeDtypeStr...  45.7 us
    pallas_call x1, Pallas kernels, local(): pl.pallas_call(finish, out_shape=(jax.ShapeDtypeStruct((rows, CONV), BF16...  2.63 us

profile of v2, /device:TPU:0, one launch (start us, length us, event | category | flops | bytes accessed | tf_op | source)
XLA Modules:
  0.0 49.0 jit_solution(8193438594917921105)
XLA Ops:
  0.6 45.7 %mixer.1 = (bf16[512,1408]{1,0:T(8,128)(2,1)}, f32[40,512]{1,0:T(8,128)}, f32[8,1408]{1,0:T(8,128)}) custom-call(bf16[512,1408]{1,0:T(8,128)(2,1)} %x_ref.1, f32[40,512]{1,0:T(8,128)} %dt_ref.1, bf16[512,1280]{1,0:T(8,128)(2,1)} %cot_ref.1, f32[4,1408]{1,0:T(4,128)} %w_ref.1, f32[1408]{0:T(1024)} %bias_ref.1, f32[1,40]{1,0:T(1,128)} %bitcast.3, ...), custom_call_target="tpu_custom_call" | custom-call | flops 2000000000 | bytes 5000000 | tf_op jit(solution)/shard_map/mixer/pallas_call | solution.py:483
  46.3 2.6 %finish.1 = (bf16[512,1408]{1,0:T(8,128)(2,1)}, f32[40,512]{1,0:T(8,128)}, f32[4,1408]{1,0:T(4,128)}, f32[1408]{0:T(1024)}, f32[40]{0:T(128)}, /*index=5*/f32[40]{0:T(128)}, f32[40]{0:T(128)}) custom-call(bf16[512,1408]{1,0:T(8,128)(2,1)} %get-tuple-element.10.gx_in, f32[40,512]{1,0:T(8,128)} %get-tuple-element.11.gdt_in, f32[8,1408]{1,0:T(8,128)} %get-tuple-element.12.sums), custom_call_target="tpu_custom_call" | custom-call | tf_op jit(solution)/shard_map/finish/pallas_call | solution.py:545
